TPU v7x, 32 devices: a whole 2x2x4 slice. The times are simulated.
32 devices in a mesh: groups: 2 (over y), ctx: 16 (over z, x, core).
Axes of the slice: x: 2, y: 2, z: 4, core: 2. Of those that a mesh axis runs over, the one named last changes fastest.
Arguments:
- reduced_rows: bfloat16 [8192, 1024], P(('groups', 'ctx')), parts along dimension 0, may hold values from -40 to 40
- query_weight: bfloat16 [1024, 4096], replicated, may hold values from -1 to 1
- key_matrix: bfloat16 [1024, 512], replicated, may hold values from -1 to 1
- value_matrix: bfloat16 [1024, 512], replicated, may hold values from -0.1875 to 0.1875
- doc_flags: int32 [64], P(('groups', 'ctx')), parts along dimension 0, may hold values from 0 to 1, as said below
Outputs:
- context: bfloat16 [8192, 4096], P(('groups', 'ctx')), parts along dimension 0
There are 2 independent parts, one for each index of `groups`. A program takes and returns all parts, laid end to end along the dimension named above; an argument that names none is the same for every part. Nothing has to cross between parts.
Inputs may be any that keep to these rules, and one draw needn't show every extreme that they name: `doc_flags`: tile 0 is a document of one tile; the document that begins at tile 1 holds exactly 2048 tokens; every document holds at most 2048 tokens.
All inputs are finite; a program needn't handle non-finite values.
Results may differ from a plain program's by a relative error of at most 0.012.
The roundings to bfloat16 on the way count: a program that leaves them out, or rounds other values in their place, can miss the bound.
Values may be sent and summed in bfloat16 or wider, within the bound.
A program may use at most 64 MiB of HBM per device.

v0:
```python
import math

import jax
import jax.numpy as jnp
from jax import lax
from jax.sharding import PartitionSpec as P

TILE = 128
LEVELS = 3
HEAD_WIDTH = 128


ROPE_BASE = 500000.0
NEG_FLOOR = -1e30


def passed_along(value, axis, steps):
    count = lax.axis_size(axis)
    leading, last = (max(0, -steps), min(count, count - steps))
    return lax.ppermute(value, axis, [(source, source + steps) for source in range(leading, last)])


def apply_rotary(vectors, token_positions):
    half_dim = vectors.shape[-1] // 2
    freq_idx = jnp.arange(half_dim, dtype=jnp.float32)
    frequency = ROPE_BASE ** (-2.0 * freq_idx / vectors.shape[-1])
    angles = token_positions.astype(jnp.float32)[:, None] * frequency[None, :]
    cosine = jnp.cos(angles)[:, None, :]
    sine_vals = jnp.sin(angles)[:, None, :]
    front_half = vectors[..., :half_dim]
    back_half = vectors[..., half_dim:]
    return jnp.concatenate(
        [front_half * cosine - back_half * sine_vals, back_half * cosine + front_half * sine_vals],
        axis=-1,
    )


def local(reduced_rows, query_weight, key_matrix, value_matrix, doc_flags):
    tok_rows = reduced_rows.shape[0]
    head_size = HEAD_WIDTH
    kv_width = key_matrix.shape[1]
    heads_kv = kv_width // head_size
    heads_q = query_weight.shape[1] // head_size
    query_group_size = heads_q // heads_kv
    device = lax.axis_index("ctx")
    first_pos = device * tok_rows
    tiles_dev = doc_flags.shape[0]
    tile_ids = device * tiles_dev + jnp.arange(tiles_dev, dtype=jnp.int32)
    local_run = lax.cummax(jnp.where(doc_flags == 1, tile_ids, -1), axis=0)
    window_max = local_run[-1:]
    incoming = None
    for level_idx in range(LEVELS + 1):
        hop_size = 1 if level_idx == 0 else 2 ** (level_idx - 1)
        arrived_mark = passed_along(window_max, "ctx", hop_size)
        if level_idx == 0:
            window_max = arrived_mark
        else:
            window_max = jnp.maximum(window_max, arrived_mark)
    incoming = window_max
    tile_start = jnp.maximum(local_run, incoming)
    doc_start = jnp.repeat(tile_start * TILE, TILE, total_repeat_length=tok_rows)
    token_positions = first_pos + jnp.arange(tok_rows, dtype=jnp.int32)
    query_rows = apply_rotary(
        jnp.dot(reduced_rows, query_weight, preferred_element_type=jnp.float32).reshape(
            tok_rows, heads_q, head_size
        ),
        token_positions,
    )
    query_rows = query_rows.astype(jnp.bfloat16).reshape(
        tok_rows, heads_kv, query_group_size, head_size
    )
    key_matrix_rows = apply_rotary(
        jnp.dot(reduced_rows, key_matrix, preferred_element_type=jnp.float32).reshape(
            tok_rows, heads_kv, head_size
        ),
        token_positions,
    )
    key_matrix_rows = key_matrix_rows.astype(jnp.bfloat16).reshape(tok_rows, kv_width)
    value_matrix_rows = jnp.dot(
        reduced_rows, value_matrix, preferred_element_type=jnp.float32
    ).astype(jnp.bfloat16)
    packed = jnp.concatenate([key_matrix_rows, value_matrix_rows], axis=1)
    score_scale = 1.0 / math.sqrt(head_size)

    def update(carry_state, slab_rows, slab_start):
        row_top, row_total, mixed_sum = carry_state
        key_slab = slab_rows[:, :kv_width].reshape(tok_rows, heads_kv, head_size)
        value_slab = slab_rows[:, kv_width:].reshape(tok_rows, heads_kv, head_size)
        key_pos = slab_start + jnp.arange(tok_rows, dtype=jnp.int32)
        visible = (key_pos[None, :] <= token_positions[:, None]) & (
            key_pos[None, :] >= doc_start[:, None]
        )
        scores = (
            jnp.einsum("qhgd,khd->hgqk", query_rows, key_slab, preferred_element_type=jnp.float32)
            * score_scale
        )
        masked = jnp.where(visible, scores, NEG_FLOOR)
        new_top = jnp.maximum(row_top, jnp.max(masked, axis=-1))
        factor = jnp.exp(row_top - new_top)
        weights = jnp.where(visible, jnp.exp(masked - new_top[..., None]), 0.0)
        row_total = row_total * factor + jnp.sum(weights, axis=-1)
        mixed_sum = mixed_sum * factor[..., None] + jnp.einsum(
            "hgqk,khd->hgqd",
            weights.astype(jnp.bfloat16),
            value_slab,
            preferred_element_type=jnp.float32,
        )
        return (new_top, row_total, mixed_sum)

    def attend(carry_state, kv_block, block_offset):
        slab_start = block_offset + 0
        carry_state = update(carry_state, kv_block, slab_start)
        return carry_state

    start_state = (
        jnp.full((heads_kv, query_group_size, tok_rows), NEG_FLOOR, jnp.float32),
        jnp.zeros((heads_kv, query_group_size, tok_rows), jnp.float32),
        jnp.zeros((heads_kv, query_group_size, tok_rows, head_size), jnp.float32),
    )
    carry_state = attend(start_state, packed, first_pos)
    back_devs = 2**LEVELS - 1

    def relay_step(step_idx, carry_pair):
        current, moving = carry_pair
        moving = passed_along(moving, "ctx", 1)
        return (attend(current, moving, first_pos - (step_idx + 1) * tok_rows), moving)

    carry_state, moving = lax.fori_loop(0, back_devs, relay_step, (carry_state, packed))
    row_top, row_total, mixed_sum = carry_state
    context = mixed_sum / row_total[..., None]
    return (
        jnp.transpose(context, (2, 0, 1, 3))
        .reshape(tok_rows, heads_q * head_size)
        .astype(jnp.bfloat16)
    )


def solution(mesh):
    in_specs = (P(("groups", "ctx"), None), P(), P(), P(), P(("groups", "ctx")))
    out_specs = P(("groups", "ctx"), None)
    return jax.shard_map(local, mesh=mesh, in_specs=in_specs, out_specs=out_specs, check_vma=False)
```

profile of v0, /device:TPU:24, one launch (start us, length us, event | category | flops | bytes accessed | tf_op | source)
XLA Modules:
  0.0 215.8 jit_solution(15741305654259436723)
XLA Ops:
  1.6 1.9 collective-permute-start.1
  5.8 1.8 fusion.48
  10.4 5.7 %convolution_bitcast_fusion = f32[32,8,32,128]{3,1,2,0:T(8,128)S(1)} fusion(bf16[256,1024]{1,0:T(8,128)(2,1)S(1)} %copy-done.3, bf16[1024,4096]{1,0:T(8,128)(2,1)} %param.10), kind=kOutput, calls=%fused_computation.43 | convolution fusion | flops 2147483648 | bytes 13107200 | tf_op jit(solution)/shard_map/dot_general | solution.py:64
  21.3 3.5 %collective-permute-start.2 = (s32[1]{0:T(128)}, s32[1]{0:T(128)}, u32[]{:S(2)}, u32[]{:S(2)}) collective-permute-start(s32[1]{0:T(128)} %collective-permute-done.1), channel_id=1, source_target_pairs={{0,1},{1,2},{2,3},{3,4},{4,5},{5,6},{6,7},{7,8},{8,9},{9,10},{10,1... | collective-permute-start | bytes 20 | tf_op jit(solution)/shard_map/ppermute | solution.py:20
  24.8 2.4 %collective-permute-done.2 = s32[1]{0:T(128)} collective-permute-done((s32[1]{0:T(128)}, s32[1]{0:T(128)}, u32[]{:S(2)}, u32[]{:S(2)}) %collective-permute-start.2) | collective-permute-done | bytes 36 | tf_op jit(solution)/shard_map/ppermute | solution.py:20
  28.4 3.8 %collective-permute-start.3 = (s32[1]{0:T(128)}, s32[1]{0:T(128)}, u32[]{:S(2)}, u32[]{:S(2)}) collective-permute-start(s32[1]{0:T(128)} %max.27), channel_id=1, source_target_pairs={{0,2},{1,3},{2,4},{3,5},{4,6},{5,7},{6,8},{7,9},{8,10},{9,11},{10,... | collective-permute-start | bytes 20 | tf_op jit(solution)/shard_map/ppermute | solution.py:20
  32.2 2.7 %collective-permute-done.3 = s32[1]{0:T(128)} collective-permute-done((s32[1]{0:T(128)}, s32[1]{0:T(128)}, u32[]{:S(2)}, u32[]{:S(2)}) %collective-permute-start.3) | collective-permute-done | bytes 36 | tf_op jit(solution)/shard_map/ppermute | solution.py:20
  36.9 4.1 %collective-permute-done.4 = s32[1]{0:T(128)} collective-permute-done((s32[1]{0:T(128)}, s32[1]{0:T(128)}, u32[]{:S(2)}, u32[]{:S(2)}) %collective-permute-start.4) | collective-permute-done | bytes 36 | tf_op jit(solution)/shard_map/ppermute | solution.py:20
  44.8 2.1 fusion.23
  47.0 4.7 %broadcast_add_fusion = f32[4,8,256,128]{3,2,1,0:T(8,128)} fusion(f32[4,8,256]{2,1,0:T(8,128)S(1)} %get-tuple-element.264, f32[4,256,256,8]{2,1,3,0:T(8,128)S(1)} %get-tuple-element.271, f32[4,8,256]{2,1,0:T(8,128)S(1)} %broadcast_maximum_fusion, pred[256,256]{0,1:T(8,128)(4,1)S(1)} %compare_and_fusion.1, bf16[256,4,128,1]{2,1,0,3:T(4,128)(2,1)S(1)} %bitcast.125), kind=kOutput, calls=%fused_computation.46 | convolution fusion | flops 548405248 | bytes 12976128 | tf_op jit(solution)/shard_map/hgqk,khd->hgqd/dot_general | solution.py:102
  51.7 157.6 %while.22 = (s32[]{:T(128)}, f32[4,8,256]{2,1,0:T(8,128)S(1)}, f32[4,8,256]{2,1,0:T(8,128)S(1)}, f32[4,8,256,128]{3,2,1,0:T(8,128)}, bf16[256,1024]{0,1:T(8,128)...) while((s32[]{:T(128)}, f32[4,8,256]{2,1,0:T(8,128)S(1)}, ...), condition=%wide.region_6.7_spmd.clone.clone, body=%wide.region_3.6_spmd.clone.clone.sunk | while | flops 1103319808 | bytes 74723576 | solution.py:128
  51.7 1.9 collective-permute-start
  55.1 8.4 %collective-permute-done = bf16[256,1024]{0,1:T(8,128)(2,1)} collective-permute-done((bf16[256,1024]{0,1:T(8,128)(2,1)}, bf16[256,1024]{0,1:T(8,128)(2,1)}, u32[]{:S(2)}, u32[]{:S(2)}) %collective-permute-start) | collective-permute-done | bytes 524320 | tf_op jit(solution)/shard_map/while/body/eval_jaxpr/ppermute | solution.py:20
  66.0 2.1 fusion.76
  68.2 3.7 %multiply_add_fusion.6 = f32[4,8,256,128]{3,2,1,0:T(8,128)S(1)} fusion(f32[4,8,256,128]{3,2,1,0:T(8,128)S(1)} %copy-done.1, f32[4,8,256]{2,1,0:T(8,128)S(1)} %get-tuple-element.343, bf16[256,4,128,1]{0,2,3,1:T(8,128)(2,1)S(1)} %bitcast.123, f32[4,256,256,8]{2,1,3,0:T(8,128)S(1)} %get-tuple-element.341, f32[4,8,256]{2,1,0:T(8,128)S(1)} %max.38, ...), kind=kOutput, calls=%fused_computation.8.clone.1 | convolution fusion | flops 549453824 | bytes 17170432 | tf_op jit(solution)/shard_map/while/body/eval_jaxpr/hgqk,khd->hgqd/dot_general | solution.py:102
  72.0 2.2 %copy.65 = bf16[256,1024]{0,1:T(8,128)(2,1)} copy(bf16[256,1024]{0,1:T(8,128)(2,1)} %collective-permute-done) | data formatting | bytes 1048576 | tf_op jit(solution)/shard_map/while
  74.2 1.9 collective-permute-start
  77.6 8.4 %collective-permute-done = bf16[256,1024]{0,1:T(8,128)(2,1)} collective-permute-done((bf16[256,1024]{0,1:T(8,128)(2,1)}, bf16[256,1024]{0,1:T(8,128)(2,1)}, u32[]{:S(2)}, u32[]{:S(2)}) %collective-permute-start) | collective-permute-done | bytes 524320 | tf_op jit(solution)/shard_map/while/body/eval_jaxpr/ppermute | solution.py:20
  88.6 2.1 fusion.76
  90.7 3.7 %multiply_add_fusion.6 = f32[4,8,256,128]{3,2,1,0:T(8,128)S(1)} fusion(f32[4,8,256,128]{3,2,1,0:T(8,128)S(1)} %copy-done.1, f32[4,8,256]{2,1,0:T(8,128)S(1)} %get-tuple-element.343, bf16[256,4,128,1]{0,2,3,1:T(8,128)(2,1)S(1)} %bitcast.123, f32[4,256,256,8]{2,1,3,0:T(8,128)S(1)} %get-tuple-element.341, f32[4,8,256]{2,1,0:T(8,128)S(1)} %max.38, ...), kind=kOutput, calls=%fused_computation.8.clone.1 | convolution fusion | flops 549453824 | bytes 17170432 | tf_op jit(solution)/shard_map/while/body/eval_jaxpr/hgqk,khd->hgqd/dot_general | solution.py:102
  94.5 2.2 %copy.65 = bf16[256,1024]{0,1:T(8,128)(2,1)} copy(bf16[256,1024]{0,1:T(8,128)(2,1)} %collective-permute-done) | data formatting | bytes 1048576 | tf_op jit(solution)/shard_map/while
  96.7 1.9 collective-permute-start
  100.1 8.4 %collective-permute-done = bf16[256,1024]{0,1:T(8,128)(2,1)} collective-permute-done((bf16[256,1024]{0,1:T(8,128)(2,1)}, bf16[256,1024]{0,1:T(8,128)(2,1)}, u32[]{:S(2)}, u32[]{:S(2)}) %collective-permute-start) | collective-permute-done | bytes 524320 | tf_op jit(solution)/shard_map/while/body/eval_jaxpr/ppermute | solution.py:20
  111.1 2.1 fusion.76
  113.2 3.7 %multiply_add_fusion.6 = f32[4,8,256,128]{3,2,1,0:T(8,128)S(1)} fusion(f32[4,8,256,128]{3,2,1,0:T(8,128)S(1)} %copy-done.1, f32[4,8,256]{2,1,0:T(8,128)S(1)} %get-tuple-element.343, bf16[256,4,128,1]{0,2,3,1:T(8,128)(2,1)S(1)} %bitcast.123, f32[4,256,256,8]{2,1,3,0:T(8,128)S(1)} %get-tuple-element.341, f32[4,8,256]{2,1,0:T(8,128)S(1)} %max.38, ...), kind=kOutput, calls=%fused_computation.8.clone.1 | convolution fusion | flops 549453824 | bytes 17170432 | tf_op jit(solution)/shard_map/while/body/eval_jaxpr/hgqk,khd->hgqd/dot_general | solution.py:102
  117.0 2.2 %copy.65 = bf16[256,1024]{0,1:T(8,128)(2,1)} copy(bf16[256,1024]{0,1:T(8,128)(2,1)} %collective-permute-done) | data formatting | bytes 1048576 | tf_op jit(solution)/shard_map/while
  119.3 1.9 collective-permute-start
  122.6 8.4 %collective-permute-done = bf16[256,1024]{0,1:T(8,128)(2,1)} collective-permute-done((bf16[256,1024]{0,1:T(8,128)(2,1)}, bf16[256,1024]{0,1:T(8,128)(2,1)}, u32[]{:S(2)}, u32[]{:S(2)}) %collective-permute-start) | collective-permute-done | bytes 524320 | tf_op jit(solution)/shard_map/while/body/eval_jaxpr/ppermute | solution.py:20
  133.6 2.1 fusion.76
  135.8 3.7 %multiply_add_fusion.6 = f32[4,8,256,128]{3,2,1,0:T(8,128)S(1)} fusion(f32[4,8,256,128]{3,2,1,0:T(8,128)S(1)} %copy-done.1, f32[4,8,256]{2,1,0:T(8,128)S(1)} %get-tuple-element.343, bf16[256,4,128,1]{0,2,3,1:T(8,128)(2,1)S(1)} %bitcast.123, f32[4,256,256,8]{2,1,3,0:T(8,128)S(1)} %get-tuple-element.341, f32[4,8,256]{2,1,0:T(8,128)S(1)} %max.38, ...), kind=kOutput, calls=%fused_computation.8.clone.1 | convolution fusion | flops 549453824 | bytes 17170432 | tf_op jit(solution)/shard_map/while/body/eval_jaxpr/hgqk,khd->hgqd/dot_general | solution.py:102
  139.5 2.2 %copy.65 = bf16[256,1024]{0,1:T(8,128)(2,1)} copy(bf16[256,1024]{0,1:T(8,128)(2,1)} %collective-permute-done) | data formatting | bytes 1048576 | tf_op jit(solution)/shard_map/while
  141.8 1.9 collective-permute-start
  145.1 8.4 %collective-permute-done = bf16[256,1024]{0,1:T(8,128)(2,1)} collective-permute-done((bf16[256,1024]{0,1:T(8,128)(2,1)}, bf16[256,1024]{0,1:T(8,128)(2,1)}, u32[]{:S(2)}, u32[]{:S(2)}) %collective-permute-start) | collective-permute-done | bytes 524320 | tf_op jit(solution)/shard_map/while/body/eval_jaxpr/ppermute | solution.py:20
  156.1 2.1 fusion.76
  158.3 3.7 %multiply_add_fusion.6 = f32[4,8,256,128]{3,2,1,0:T(8,128)S(1)} fusion(f32[4,8,256,128]{3,2,1,0:T(8,128)S(1)} %copy-done.1, f32[4,8,256]{2,1,0:T(8,128)S(1)} %get-tuple-element.343, bf16[256,4,128,1]{0,2,3,1:T(8,128)(2,1)S(1)} %bitcast.123, f32[4,256,256,8]{2,1,3,0:T(8,128)S(1)} %get-tuple-element.341, f32[4,8,256]{2,1,0:T(8,128)S(1)} %max.38, ...), kind=kOutput, calls=%fused_computation.8.clone.1 | convolution fusion | flops 549453824 | bytes 17170432 | tf_op jit(solution)/shard_map/while/body/eval_jaxpr/hgqk,khd->hgqd/dot_general | solution.py:102
  162.0 2.2 %copy.65 = bf16[256,1024]{0,1:T(8,128)(2,1)} copy(bf16[256,1024]{0,1:T(8,128)(2,1)} %collective-permute-done) | data formatting | bytes 1048576 | tf_op jit(solution)/shard_map/while
  164.3 1.9 collective-permute-start
  167.6 8.4 %collective-permute-done = bf16[256,1024]{0,1:T(8,128)(2,1)} collective-permute-done((bf16[256,1024]{0,1:T(8,128)(2,1)}, bf16[256,1024]{0,1:T(8,128)(2,1)}, u32[]{:S(2)}, u32[]{:S(2)}) %collective-permute-start) | collective-permute-done | bytes 524320 | tf_op jit(solution)/shard_map/while/body/eval_jaxpr/ppermute | solution.py:20
  178.6 2.1 fusion.76
  180.8 3.7 %multiply_add_fusion.6 = f32[4,8,256,128]{3,2,1,0:T(8,128)S(1)} fusion(f32[4,8,256,128]{3,2,1,0:T(8,128)S(1)} %copy-done.1, f32[4,8,256]{2,1,0:T(8,128)S(1)} %get-tuple-element.343, bf16[256,4,128,1]{0,2,3,1:T(8,128)(2,1)S(1)} %bitcast.123, f32[4,256,256,8]{2,1,3,0:T(8,128)S(1)} %get-tuple-element.341, f32[4,8,256]{2,1,0:T(8,128)S(1)} %max.38, ...), kind=kOutput, calls=%fused_computation.8.clone.1 | convolution fusion | flops 549453824 | bytes 17170432 | tf_op jit(solution)/shard_map/while/body/eval_jaxpr/hgqk,khd->hgqd/dot_general | solution.py:102
  184.5 2.2 %copy.65 = bf16[256,1024]{0,1:T(8,128)(2,1)} copy(bf16[256,1024]{0,1:T(8,128)(2,1)} %collective-permute-done) | data formatting | bytes 1048576 | tf_op jit(solution)/shard_map/while
  186.8 1.9 collective-permute-start
  190.1 8.4 %collective-permute-done = bf16[256,1024]{0,1:T(8,128)(2,1)} collective-permute-done((bf16[256,1024]{0,1:T(8,128)(2,1)}, bf16[256,1024]{0,1:T(8,128)(2,1)}, u32[]{:S(2)}, u32[]{:S(2)}) %collective-permute-start) | collective-permute-done | bytes 524320 | tf_op jit(solution)/shard_map/while/body/eval_jaxpr/ppermute | solution.py:20
  201.1 2.1 fusion.76
  203.3 3.7 %multiply_add_fusion.6 = f32[4,8,256,128]{3,2,1,0:T(8,128)S(1)} fusion(f32[4,8,256,128]{3,2,1,0:T(8,128)S(1)} %copy-done.1, f32[4,8,256]{2,1,0:T(8,128)S(1)} %get-tuple-element.343, bf16[256,4,128,1]{0,2,3,1:T(8,128)(2,1)S(1)} %bitcast.123, f32[4,256,256,8]{2,1,3,0:T(8,128)S(1)} %get-tuple-element.341, f32[4,8,256]{2,1,0:T(8,128)S(1)} %max.38, ...), kind=kOutput, calls=%fused_computation.8.clone.1 | convolution fusion | flops 549453824 | bytes 17170432 | tf_op jit(solution)/shard_map/while/body/eval_jaxpr/hgqk,khd->hgqd/dot_general | solution.py:102
  207.0 2.2 %copy.65 = bf16[256,1024]{0,1:T(8,128)(2,1)} copy(bf16[256,1024]{0,1:T(8,128)(2,1)} %collective-permute-done) | data formatting | bytes 1048576 | tf_op jit(solution)/shard_map/while
  209.3 2.9 %fusion.31 = bf16[256,4,8,128]{3,0,2,1:T(8,128)(2,1)S(1)} fusion(f32[4,8,256,128]{3,2,1,0:T(8,128)} %get-tuple-element.172, f32[4,8,256]{2,1,0:T(8,128)S(1)} %get-tuple-element.173), kind=kLoop, calls=%fused_computation.47 | loop fusion | flops 2097152 | bytes 6324224 | tf_op jit(solution)/shard_map/convert_element_type | solution.py:134
  213.5 2.3 %copy.50 = bf16[32,8,32,128]{3,1,2,0:T(8,128)(2,1)} copy(bf16[32,8,32,128]{3,2,1,0:T(8,128)(2,1)S(1)} %bitcast.122) | data formatting | bytes 4194304
  (145 shorter events, 45.7 us)
Async XLA Ops:
  0.0 3.5 %copy-start = (bf16[1024,512]{1,0:T(8,128)(2,1)S(1)}, bf16[1024,512]{1,0:T(8,128)(2,1)}, u32[]{:S(2)}) copy-start(bf16[1024,512]{1,0:T(8,128)(2,1)} %param.12) | copy-start | bytes 3145732
  1.6 19.7 %collective-permute-start.1 = (s32[1]{0:T(128)}, s32[1]{0:T(128)}, u32[]{:S(2)}, u32[]{:S(2)}) collective-permute-start(s32[1]{0:T(128)} %bitcast.5), channel_id=1, source_target_pairs={{0,1},{1,2},{2,3},{3,4},{4,5},{5,6},{6,7},{7,8},{8,9},{9,10},{10,1... | collective-permute-start | bytes 20 | tf_op jit(solution)/shard_map/ppermute | solution.py:20
  7.8 2.6 %copy-start.3 = (bf16[256,1024]{1,0:T(8,128)(2,1)S(1)}, bf16[256,1024]{1,0:T(8,128)(2,1)}, u32[]{:S(2)}) copy-start(bf16[256,1024]{1,0:T(8,128)(2,1)} %param.9) | copy-start | bytes 1572868
  21.3 5.9 %collective-permute-start.2 = (s32[1]{0:T(128)}, s32[1]{0:T(128)}, u32[]{:S(2)}, u32[]{:S(2)}) collective-permute-start(s32[1]{0:T(128)} %collective-permute-done.1), channel_id=1, source_target_pairs={{0,1},{1,2},{2,3},{3,4},{4,5},{5,6},{6,7},{7,8},{8,9},{9,10},{10,1... | collective-permute-start | bytes 20 | tf_op jit(solution)/shard_map/ppermute | solution.py:20
  28.4 6.4 %collective-permute-start.3 = (s32[1]{0:T(128)}, s32[1]{0:T(128)}, u32[]{:S(2)}, u32[]{:S(2)}) collective-permute-start(s32[1]{0:T(128)} %max.27), channel_id=1, source_target_pairs={{0,2},{1,3},{2,4},{3,5},{4,6},{5,7},{6,8},{7,9},{8,10},{9,11},{10,... | collective-permute-start | bytes 20 | tf_op jit(solution)/shard_map/ppermute | solution.py:20
  35.4 5.5 %collective-permute-start.4 = (s32[1]{0:T(128)}, s32[1]{0:T(128)}, u32[]{:S(2)}, u32[]{:S(2)}) collective-permute-start(s32[1]{0:T(128)} %max.28), channel_id=1, source_target_pairs={{0,4},{1,5},{2,6},{3,7},{4,8},{5,9},{6,10},{7,11},{8,12},{9,13},{1... | collective-permute-start | bytes 20 | tf_op jit(solution)/shard_map/ppermute | solution.py:20
  44.8 2.1 copy-start.4
  51.7 11.7 %collective-permute-start = (bf16[256,1024]{0,1:T(8,128)(2,1)}, bf16[256,1024]{0,1:T(8,128)(2,1)}, u32[]{:S(2)}, u32[]{:S(2)}) collective-permute-start(bf16[256,1024]{0,1:T(8,128)(2,1)} %get-tuple-element.360), channel_id=1, source_target_pairs={{0,1},{1,2},{2,3},{3,4},{4,5},{5,6},{6,7},{7,8},{8,9},{9,10},{10,1... | collective-permute-start | bytes 1572872 | tf_op jit(solution)/shard_map/while/body/eval_jaxpr/ppermute | solution.py:20
  66.0 2.2 %copy-start.1 = (f32[4,8,256,128]{3,2,1,0:T(8,128)S(1)}, f32[4,8,256,128]{3,2,1,0:T(8,128)}, u32[]{:S(2)}) copy-start(f32[4,8,256,128]{3,2,1,0:T(8,128)} %get-tuple-element.359) | copy-start | bytes 12582916 | tf_op jit(solution)/shard_map/while
  72.0 2.3 %copy-start.2 = (f32[4,8,256,128]{3,2,1,0:T(8,128)}, f32[4,8,256,128]{3,2,1,0:T(8,128)S(1)}, u32[]{:S(2)}) copy-start(f32[4,8,256,128]{3,2,1,0:T(8,128)S(1)} %multiply_add_fusion.6) | copy-start | bytes 12582916 | tf_op jit(solution)/shard_map/while
  74.2 11.7 %collective-permute-start = (bf16[256,1024]{0,1:T(8,128)(2,1)}, bf16[256,1024]{0,1:T(8,128)(2,1)}, u32[]{:S(2)}, u32[]{:S(2)}) collective-permute-start(bf16[256,1024]{0,1:T(8,128)(2,1)} %get-tuple-element.360), channel_id=1, source_target_pairs={{0,1},{1,2},{2,3},{3,4},{4,5},{5,6},{6,7},{7,8},{8,9},{9,10},{10,1... | collective-permute-start | bytes 1572872 | tf_op jit(solution)/shard_map/while/body/eval_jaxpr/ppermute | solution.py:20
  88.5 2.2 %copy-start.1 = (f32[4,8,256,128]{3,2,1,0:T(8,128)S(1)}, f32[4,8,256,128]{3,2,1,0:T(8,128)}, u32[]{:S(2)}) copy-start(f32[4,8,256,128]{3,2,1,0:T(8,128)} %get-tuple-element.359) | copy-start | bytes 12582916 | tf_op jit(solution)/shard_map/while
  94.5 2.3 %copy-start.2 = (f32[4,8,256,128]{3,2,1,0:T(8,128)}, f32[4,8,256,128]{3,2,1,0:T(8,128)S(1)}, u32[]{:S(2)}) copy-start(f32[4,8,256,128]{3,2,1,0:T(8,128)S(1)} %multiply_add_fusion.6) | copy-start | bytes 12582916 | tf_op jit(solution)/shard_map/while
  96.7 11.7 %collective-permute-start = (bf16[256,1024]{0,1:T(8,128)(2,1)}, bf16[256,1024]{0,1:T(8,128)(2,1)}, u32[]{:S(2)}, u32[]{:S(2)}) collective-permute-start(bf16[256,1024]{0,1:T(8,128)(2,1)} %get-tuple-element.360), channel_id=1, source_target_pairs={{0,1},{1,2},{2,3},{3,4},{4,5},{5,6},{6,7},{7,8},{8,9},{9,10},{10,1... | collective-permute-start | bytes 1572872 | tf_op jit(solution)/shard_map/while/body/eval_jaxpr/ppermute | solution.py:20
  111.0 2.2 %copy-start.1 = (f32[4,8,256,128]{3,2,1,0:T(8,128)S(1)}, f32[4,8,256,128]{3,2,1,0:T(8,128)}, u32[]{:S(2)}) copy-start(f32[4,8,256,128]{3,2,1,0:T(8,128)} %get-tuple-element.359) | copy-start | bytes 12582916 | tf_op jit(solution)/shard_map/while
  117.0 2.3 %copy-start.2 = (f32[4,8,256,128]{3,2,1,0:T(8,128)}, f32[4,8,256,128]{3,2,1,0:T(8,128)S(1)}, u32[]{:S(2)}) copy-start(f32[4,8,256,128]{3,2,1,0:T(8,128)S(1)} %multiply_add_fusion.6) | copy-start | bytes 12582916 | tf_op jit(solution)/shard_map/while
  119.3 11.7 %collective-permute-start = (bf16[256,1024]{0,1:T(8,128)(2,1)}, bf16[256,1024]{0,1:T(8,128)(2,1)}, u32[]{:S(2)}, u32[]{:S(2)}) collective-permute-start(bf16[256,1024]{0,1:T(8,128)(2,1)} %get-tuple-element.360), channel_id=1, source_target_pairs={{0,1},{1,2},{2,3},{3,4},{4,5},{5,6},{6,7},{7,8},{8,9},{9,10},{10,1... | collective-permute-start | bytes 1572872 | tf_op jit(solution)/shard_map/while/body/eval_jaxpr/ppermute | solution.py:20
  133.6 2.2 %copy-start.1 = (f32[4,8,256,128]{3,2,1,0:T(8,128)S(1)}, f32[4,8,256,128]{3,2,1,0:T(8,128)}, u32[]{:S(2)}) copy-start(f32[4,8,256,128]{3,2,1,0:T(8,128)} %get-tuple-element.359) | copy-start | bytes 12582916 | tf_op jit(solution)/shard_map/while
  139.5 2.3 %copy-start.2 = (f32[4,8,256,128]{3,2,1,0:T(8,128)}, f32[4,8,256,128]{3,2,1,0:T(8,128)S(1)}, u32[]{:S(2)}) copy-start(f32[4,8,256,128]{3,2,1,0:T(8,128)S(1)} %multiply_add_fusion.6) | copy-start | bytes 12582916 | tf_op jit(solution)/shard_map/while
  141.8 11.7 %collective-permute-start = (bf16[256,1024]{0,1:T(8,128)(2,1)}, bf16[256,1024]{0,1:T(8,128)(2,1)}, u32[]{:S(2)}, u32[]{:S(2)}) collective-permute-start(bf16[256,1024]{0,1:T(8,128)(2,1)} %get-tuple-element.360), channel_id=1, source_target_pairs={{0,1},{1,2},{2,3},{3,4},{4,5},{5,6},{6,7},{7,8},{8,9},{9,10},{10,1... | collective-permute-start | bytes 1572872 | tf_op jit(solution)/shard_map/while/body/eval_jaxpr/ppermute | solution.py:20
  156.1 2.2 %copy-start.1 = (f32[4,8,256,128]{3,2,1,0:T(8,128)S(1)}, f32[4,8,256,128]{3,2,1,0:T(8,128)}, u32[]{:S(2)}) copy-start(f32[4,8,256,128]{3,2,1,0:T(8,128)} %get-tuple-element.359) | copy-start | bytes 12582916 | tf_op jit(solution)/shard_map/while
  162.0 2.3 %copy-start.2 = (f32[4,8,256,128]{3,2,1,0:T(8,128)}, f32[4,8,256,128]{3,2,1,0:T(8,128)S(1)}, u32[]{:S(2)}) copy-start(f32[4,8,256,128]{3,2,1,0:T(8,128)S(1)} %multiply_add_fusion.6) | copy-start | bytes 12582916 | tf_op jit(solution)/shard_map/while
  164.3 11.7 %collective-permute-start = (bf16[256,1024]{0,1:T(8,128)(2,1)}, bf16[256,1024]{0,1:T(8,128)(2,1)}, u32[]{:S(2)}, u32[]{:S(2)}) collective-permute-start(bf16[256,1024]{0,1:T(8,128)(2,1)} %get-tuple-element.360), channel_id=1, source_target_pairs={{0,1},{1,2},{2,3},{3,4},{4,5},{5,6},{6,7},{7,8},{8,9},{9,10},{10,1... | collective-permute-start | bytes 1572872 | tf_op jit(solution)/shard_map/while/body/eval_jaxpr/ppermute | solution.py:20
  178.6 2.2 %copy-start.1 = (f32[4,8,256,128]{3,2,1,0:T(8,128)S(1)}, f32[4,8,256,128]{3,2,1,0:T(8,128)}, u32[]{:S(2)}) copy-start(f32[4,8,256,128]{3,2,1,0:T(8,128)} %get-tuple-element.359) | copy-start | bytes 12582916 | tf_op jit(solution)/shard_map/while
  184.5 2.3 %copy-start.2 = (f32[4,8,256,128]{3,2,1,0:T(8,128)}, f32[4,8,256,128]{3,2,1,0:T(8,128)S(1)}, u32[]{:S(2)}) copy-start(f32[4,8,256,128]{3,2,1,0:T(8,128)S(1)} %multiply_add_fusion.6) | copy-start | bytes 12582916 | tf_op jit(solution)/shard_map/while
  186.8 11.7 %collective-permute-start = (bf16[256,1024]{0,1:T(8,128)(2,1)}, bf16[256,1024]{0,1:T(8,128)(2,1)}, u32[]{:S(2)}, u32[]{:S(2)}) collective-permute-start(bf16[256,1024]{0,1:T(8,128)(2,1)} %get-tuple-element.360), channel_id=1, source_target_pairs={{0,1},{1,2},{2,3},{3,4},{4,5},{5,6},{6,7},{7,8},{8,9},{9,10},{10,1... | collective-permute-start | bytes 1572872 | tf_op jit(solution)/shard_map/while/body/eval_jaxpr/ppermute | solution.py:20
  201.1 2.2 %copy-start.1 = (f32[4,8,256,128]{3,2,1,0:T(8,128)S(1)}, f32[4,8,256,128]{3,2,1,0:T(8,128)}, u32[]{:S(2)}) copy-start(f32[4,8,256,128]{3,2,1,0:T(8,128)} %get-tuple-element.359) | copy-start | bytes 12582916 | tf_op jit(solution)/shard_map/while
  207.0 2.3 %copy-start.2 = (f32[4,8,256,128]{3,2,1,0:T(8,128)}, f32[4,8,256,128]{3,2,1,0:T(8,128)S(1)}, u32[]{:S(2)}) copy-start(f32[4,8,256,128]{3,2,1,0:T(8,128)S(1)} %multiply_add_fusion.6) | copy-start | bytes 12582916 | tf_op jit(solution)/shard_map/while
where the time goes:
time: 217 us; the launch traced here: 216 us
  waiting for transfers between devices  67.7 us (31%)
  matrix products  51.8 us (24%)
  other arithmetic  35.6 us (16%)
  local copies, waits for them, and re-layouts  33.1 us (15%)
  starting transfers between devices  24 us (11%)
  between operations  2.57 us (1%)
    ppermute x11, waiting for transfers between devices, passed_along(): lax.ppermute(value, axis, [(source, source + steps) for source in range(l...  67.7 us
    dot_general x8, matrix products, update(): jnp.einsum('hgqk,khd->hgqd', weights.astype(jnp.bfloat16), value_slab, pr...  30.9 us
    ppermute x11, starting transfers between devices, passed_along(): lax.ppermute(value, axis, [(source, source + steps) for source in range(l...  24 us
    reduce_sum x8, other arithmetic, update(): row_total = row_total * factor + jnp.sum(weights, axis=-1)  17 us
    while x42, local copies, waits for them, and re-layouts  15.8 us
    dot_general x8, matrix products, update(): jnp.einsum('qhgd,khd->hgqk', query_rows, key_slab, preferred_element_type...  11.9 us
    gather x8, other arithmetic, local(): jnp.repeat(tile_start * TILE, TILE, total_repeat_length=tok_rows)  9.75 us
    slice x7, local copies, waits for them, and re-layouts, update(): value_slab = slab_rows[:, kv_width:].reshape(tok_rows, heads_kv, head_size)  7.45 us
  transfers between devices with their start and end apart: 11, of which 10 were waited for; matrix products, arithmetic and copies ran while one was open for 13% of the time, Pallas kernels for 0%

commit v1 on v0

v1 whole, which is shorter than its diff:
```python
import functools
import math

import jax
import jax.numpy as jnp
import numpy as np
from jax import lax
from jax.experimental import pallas as pl
from jax.experimental.pallas import tpu as pltpu

TILE = 128
MAXDOC = 2048
HEAD = 128
ROPE_BASE = 500000.0
NEG = -1e30
MARK_ROWS = 16


def needed(source, target):
    edge = MAXDOC // TILE // 4
    return (source >= 0) & ((source >= edge) | (target <= edge))


def kernel(
    chips, group, flags_ref, x_ref, wk_ref, wv_ref, cos_ref, sin_ref, freq_ref, wq_hbm, out_hbm,
    kv, send, xs, wq, queries, top, mix, bias_own, blocked, staged, cosine, sine,
    wq_sem, x_send, x_recv, kv_send, kv_recv, out_sem, out_send, out_recv,
):
    me = lax.axis_index("ctx")
    chip, core = me // 2, me % 2
    other = 1 - core
    sibling = chip * 2 + other
    tok = x_ref.shape[0]
    half = wq.shape[1]
    scale = math.log2(math.e) / math.sqrt(HEAD)

    wq_copy = pltpu.make_async_copy(
        wq_hbm.at[:, pl.ds(pl.multiple_of(core * half, half), half)], wq, wq_sem
    )
    wq_copy.start()

    barrier = pltpu.get_barrier_semaphore()
    pl.semaphore_signal(barrier, inc=1, device_id={"ctx": sibling})
    for hop in range(1, 5):
        @pl.when(needed(chip - hop, chip))
        def _():
            for c in range(2) if hop < 4 else (1,):
                pl.semaphore_signal(barrier, inc=1, device_id={"ctx": (chip - hop) * 2 + c})

    def sends_to(hop):
        fits = (chip + hop < chips) & needed(chip, chip + hop)
        return fits if hop < 4 else fits & (core == 1)

    base = (chip * (2 * tok)).astype(jnp.float32) * freq_ref[...]
    cos_b, sin_b = jnp.cos(base)[:1], jnp.sin(base)[:1]
    sign = jnp.where(lax.broadcasted_iota(jnp.int32, (1, HEAD), 1) < HEAD // 2, -1.0, 1.0)
    cosine[...] = cos_ref[...] * cos_b - sin_ref[...] * sin_b
    sine[...] = (sin_ref[...] * cos_b + cos_ref[...] * sin_b) * sign

    def rope(v, cs, sn):
        return v * cs + pltpu.roll(v, HEAD // 2, 1) * sn

    own = pl.ds(pl.multiple_of(core * tok, tok), tok)
    x = x_ref[...]
    cs, sn = cosine[own, :], sine[own, :]
    heads = wk_ref.shape[1] // HEAD // 2
    flag_rows = jnp.where(
        lax.broadcasted_iota(jnp.int32, (MARK_ROWS, HEAD), 0) < MARK_ROWS // 2, flags_ref[0], flags_ref[1]
    ).astype(jnp.float32).astype(jnp.bfloat16)
    for part in range(2):
        cols = slice(part * heads * HEAD, (part + 1) * heads * HEAD)
        ks = jnp.dot(x, wk_ref[:, cols], preferred_element_type=jnp.float32)
        vs = jnp.dot(x, wv_ref[:, cols], preferred_element_type=jnp.float32)
        for h in range(heads):
            hc = slice(h * HEAD, (h + 1) * HEAD)
            send[part, 2 * h * tok:(2 * h + 1) * tok, :] = rope(ks[:, hc], cs, sn).astype(jnp.bfloat16)
            send[part, (2 * h + 1) * tok:(2 * h + 2) * tok, :] = vs[:, hc].astype(jnp.bfloat16)
        send[part, 2 * heads * tok:, :] = flag_rows

    targets = sum(sends_to(hop).astype(jnp.int32) for hop in range(1, 5))
    pl.semaphore_wait(barrier, 1 + 2 * targets)

    def kv_copy(hop, part):
        return pltpu.make_async_remote_copy(
            src_ref=send.at[part], dst_ref=kv.at[hop, core],
            send_sem=kv_send.at[hop, part], recv_sem=kv_recv.at[hop, core],
            device_id={"ctx": (chip + hop) * 2 + part},
        )

    def own_copy():
        return pltpu.make_async_remote_copy(
            src_ref=send.at[other], dst_ref=kv.at[0, core],
            send_sem=kv_send.at[0, 0], recv_sem=kv_recv.at[0, core],
            device_id={"ctx": sibling},
        )

    x_copy = pltpu.make_async_remote_copy(
        src_ref=x_ref, dst_ref=xs.at[core], send_sem=x_send, recv_sem=x_recv, device_id={"ctx": sibling},
    )
    x_copy.start()
    own_copy().start()
    for hop in range(1, 5):
        @pl.when(sends_to(hop))
        def _():
            for part in range(2):
                kv_copy(hop, part).start()
    xs[core] = x
    kv[0, core] = send[core]

    x_copy.wait()
    wq_copy.wait()
    pairs = half // (2 * HEAD)
    tiles = 2 * tok // TILE

    @pl.loop(0, pairs)
    def _(pair):
        kvh, hp = pair // (group // 2), pair % (group // 2)
        w = wq[:, pl.ds(pl.multiple_of(pair * 2 * HEAD, 2 * HEAD), 2 * HEAD)]
        for c in range(2):
            q = jnp.dot(xs[c], w, preferred_element_type=jnp.float32)
            for e in range(2):
                r = rope(
                    q[:, e * HEAD:(e + 1) * HEAD], cosine[c * tok:(c + 1) * tok, :], sine[c * tok:(c + 1) * tok, :]
                ).astype(jnp.bfloat16)
                for t in range(tok // TILE):
                    queries[
                        kvh, c * (tok // TILE) + t, pl.ds(pl.multiple_of((hp * 2 + e) * TILE, TILE), TILE), :
                    ] = r[t * TILE:(t + 1) * TILE]

    def marks(hop, c):
        rows = kv[hop, c, 2 * heads * tok:, :].astype(jnp.float32)
        return [rows[0:1], rows[MARK_ROWS // 2:MARK_ROWS // 2 + 1]]

    chunk = 2 * TILE

    def attend(hop, unit_tiles, cores, bias_of, first):
        @pl.loop(0, heads * unit_tiles)
        def _(unit):
            h, i = unit // unit_tiles, unit % unit_tiles
            k0 = pl.multiple_of(h * 2 * tok, tok)
            v0 = pl.multiple_of(h * 2 * tok + tok, tok)
            k = jnp.concatenate([kv[hop, c, pl.ds(k0, tok), :] for c in cores], axis=0)
            v = jnp.concatenate([kv[hop, c, pl.ds(v0, tok), :] for c in cores], axis=0)
            v = jnp.concatenate([v, jnp.ones_like(v)], axis=1)
            bias = bias_of(i)
            for r in range(group * TILE // chunk):
                rows = slice(r * chunk, (r + 1) * chunk)
                s = lax.dot_general(
                    queries[h, i, rows, :], k, (((1,), (1,)), ((), ())), preferred_element_type=jnp.float32
                )
                s = s + bias
                highest = jnp.max(s, axis=1, keepdims=True)
                if first:
                    new = jnp.broadcast_to(highest, (chunk, HEAD))
                else:
                    old = top[h, i, rows, :]
                    new = jnp.maximum(old, highest)
                wide = jnp.concatenate([new] * (s.shape[1] // HEAD), axis=1)
                p = jnp.exp2((s - wide) * scale).astype(jnp.bfloat16)
                o = jnp.dot(p, v, preferred_element_type=jnp.float32)
                if not first:
                    factor = jnp.exp2((old - new) * scale)
                    o = o + mix[h, i, rows, :] * jnp.concatenate([factor, factor], axis=1)
                mix[h, i, rows, :] = o
                top[h, i, rows, :] = new

    own_copy().wait_send()
    pltpu.make_async_remote_copy(
        src_ref=send.at[other], dst_ref=kv.at[0, other], send_sem=kv_send.at[0, 0],
        recv_sem=kv_recv.at[0, other], device_id={"ctx": sibling},
    ).wait_recv()
    flags = marks(0, 0) + marks(0, 1)
    row = lax.broadcasted_iota(jnp.int32, (TILE, TILE), 0)
    col = lax.broadcasted_iota(jnp.int32, (TILE, TILE), 1)
    causal = jnp.where(col <= row, 0.0, NEG)
    for i in range(tiles):
        seen = jnp.zeros((1, HEAD), jnp.float32)
        for j in reversed(range(tiles)):
            cols = slice(j * TILE, (j + 1) * TILE)
            if j > i:
                bias_own[i, :, cols] = jnp.full((TILE, TILE), NEG, jnp.float32)
            elif j == i:
                bias_own[i, :, cols] = causal
                seen = flags[j]
            else:
                bias_own[i, :, cols] = jnp.broadcast_to(seen * NEG, (TILE, TILE))
                seen = jnp.maximum(seen, flags[j])
        blocked[i] = jnp.broadcast_to(seen, (8, HEAD))

    def own_bias(i):
        b = bias_own[i]
        return jnp.concatenate([b] * (chunk // TILE), axis=0)

    attend(0, tiles, (0, 1), own_bias, True)

    def far_bias(i, cores, hop):
        seen = blocked[i][0:1]
        cols = []
        for c in reversed(cores):
            for f in reversed(marks(hop, c)):
                cols.insert(0, seen * NEG)
                seen = jnp.maximum(seen, f)
        return jnp.concatenate(cols, axis=1), seen

    for hop in range(1, 5):
        cores = (0, 1) if hop < 4 else (1,)
        unit_tiles = tiles if hop < 4 else tiles // 2

        @pl.when(needed(chip - hop, chip))
        def _():
            for c in cores:
                pltpu.make_async_remote_copy(
                    src_ref=send.at[0], dst_ref=kv.at[hop, c], send_sem=kv_send.at[hop, 0],
                    recv_sem=kv_recv.at[hop, c], device_id={"ctx": sibling},
                ).wait_recv()
            attend(hop, unit_tiles, cores, lambda i: far_bias(i, cores, hop)[0], False)
            if hop < 4:
                for i in range(tiles):
                    blocked[i] = jnp.broadcast_to(far_bias(i, cores, hop)[1], (8, HEAD))

    @pl.loop(0, heads * tiles)
    def _(unit):
        h, i = unit // tiles, unit % tiles
        for r in range(group):
            rows = slice(r * TILE, (r + 1) * TILE)
            a = mix[h, i, rows, :]
            staged[
                pl.ds(pl.multiple_of(i * TILE, TILE), TILE),
                pl.ds(pl.multiple_of((h * group + r) * HEAD, HEAD), HEAD),
            ] = (a[:, :HEAD] / a[:, HEAD:]).astype(jnp.bfloat16)

    my_cols = pl.ds(pl.multiple_of(core * half, half), half)
    their_rows = pl.ds(pl.multiple_of(other * tok, tok), tok)
    out_remote = pltpu.make_async_remote_copy(
        src_ref=staged.at[their_rows, :], dst_ref=out_hbm.at[:, my_cols],
        send_sem=out_send, recv_sem=out_recv, device_id={"ctx": sibling},
    )
    out_remote.start()
    out_local = pltpu.make_async_copy(staged.at[own, :], out_hbm.at[:, my_cols], out_sem)
    out_local.start()
    for hop in range(1, 5):
        @pl.when(sends_to(hop))
        def _():
            for part in range(2):
                kv_copy(hop, part).wait_send()
    out_local.wait()
    out_remote.wait()


def local(chips, reduced_rows, query_weight, key_matrix, value_matrix, doc_flags):
    tok, rank = reduced_rows.shape
    q_width = query_weight.shape[1]
    kv_heads = key_matrix.shape[1] // HEAD
    group = q_width // HEAD // kv_heads
    half, heads = q_width // 2, kv_heads // 2
    tiles = 2 * tok // TILE
    slab = 2 * heads * tok + MARK_ROWS
    m = np.arange(HEAD // 2, dtype=np.float64)
    freq = ROPE_BASE ** (-2.0 * m / HEAD)
    freq = np.concatenate([freq, freq])
    angles = np.arange(2 * tok, dtype=np.float64)[:, None] * freq[None, :]
    vmem = pl.BlockSpec(memory_space=pltpu.VMEM)
    bf, f32 = jnp.bfloat16, jnp.float32
    dma = pltpu.SemaphoreType.DMA
    return pl.pallas_call(
        functools.partial(kernel, chips, group),
        out_shape=jax.ShapeDtypeStruct((tok, q_width), bf),
        in_specs=[pl.BlockSpec(memory_space=pltpu.SMEM)] + [vmem] * 6 + [pl.BlockSpec(memory_space=pl.ANY)],
        out_specs=pl.BlockSpec(memory_space=pl.ANY),
        scratch_shapes=[
            pltpu.VMEM((5, 2, slab, HEAD), bf),
            pltpu.VMEM((2, slab, HEAD), bf),
            pltpu.VMEM((2, tok, rank), bf),
            pltpu.VMEM((rank, half), bf),
            pltpu.VMEM((heads, tiles, group * TILE, HEAD), bf),
            pltpu.VMEM((heads, tiles, group * TILE, HEAD), f32),
            pltpu.VMEM((heads, tiles, group * TILE, 2 * HEAD), f32),
            pltpu.VMEM((tiles, TILE, tiles * TILE), f32),
            pltpu.VMEM((tiles, 8, HEAD), f32),
            pltpu.VMEM((2 * tok, half), bf),
            pltpu.VMEM((2 * tok, HEAD), f32),
            pltpu.VMEM((2 * tok, HEAD), f32),
            dma, dma, dma, dma((5, 2)), dma((5, 2)), dma, dma, dma,
        ],
        compiler_params=pltpu.CompilerParams(
            collective_id=0, has_side_effects=True, vmem_limit_bytes=56 * 1024 * 1024
        ),
        cost_estimate=pl.CostEstimate(flops=12 * 10**9, bytes_accessed=12 * 10**6, transcendentals=16 * 10**6),
    )(
        doc_flags, reduced_rows, key_matrix, value_matrix,
        jnp.asarray(np.cos(angles), f32), jnp.asarray(np.sin(angles), f32),
        jnp.asarray(np.broadcast_to(freq, (8, HEAD)), f32), query_weight,
    )


def solution(mesh):
    chips = mesh.shape["ctx"] // 2
    in_specs = (P(("groups", "ctx"), None), P(), P(), P(), P(("groups", "ctx")))
    return jax.shard_map(
        functools.partial(local, chips), mesh=mesh, in_specs=in_specs,
        out_specs=P(("groups", "ctx"), None), check_vma=False,
    )


P = jax.sharding.PartitionSpec
```

time: 217 us -> 58.1 us (0.27)
  the two profiles are of different devices: /device:TPU:24 before, /device:TPU:17 now
where the time goes in v1:
time: 58.1 us; the launch traced here: 58 us
  Pallas kernels  54.8 us (94%)
  local copies, waits for them, and re-layouts  3.13 us (5%)
    pallas_call x1, Pallas kernels, local(): pl.pallas_call(functools.partial(kernel, chips, group), out_shape=jax.Sha...  54.8 us
    unnamed x1, local copies, waits for them, and re-layouts  3.13 us

profile of v1, /device:TPU:17, one launch (start us, length us, event | category | flops | bytes accessed | tf_op | source)
XLA Modules:
  0.0 58.0 jit_solution(14567696453992755285)
XLA Ops:
  0.0 54.8 %shard_map.82 = bf16[256,4096]{1,0:T(8,128)(2,1)} custom-call(s32[2]{0:T(128)} %flags_ref.1, bf16[256,1024]{1,0:T(8,128)(2,1)} %x_ref.1, bf16[1024,512]{1,0:T(8,128)(2,1)} %wk_ref.1, bf16[1024,512]{1,0:T(8,128)(2,1)} %wv_ref.1, f32[512,128]{1,0:T(8,128)} %constant.6.clone.cos_ref, f32[512,128]{1,0:T(8,128)} %constant.7.clone.sin_ref, ...), custom_call_target="tpu_custom_call" | custom-call | flops 12000000000 | bytes 12000000 | tf_op jit(solution)/shard_map/pallas_call | solution.py:265
  54.8 3.1 %copy.10 = bf16[256,4096]{1,0:T(8,128)(2,1)} copy(bf16[256,4096]{1,0:T(8,128)(2,1)} %shard_map.82) | data formatting | bytes 4194304

commit v2 on v1

--- a/solution.py
+++ b/solution.py
@@ -13,18 +13,29 @@
 HEAD = 128
 ROPE_BASE = 500000.0
 NEG = -1e30
+CHUNK = 256
+AHEAD = 1
 MARK_ROWS = 16
+RELAY = 2
 
 
 def needed(source, target):
-    edge = MAXDOC // TILE // 4
-    return (source >= 0) & ((source >= edge) | (target <= edge))
+    return (source >= 0) & ((source >= EDGE) | (target <= EDGE))
+
+
+EDGE = MAXDOC // TILE // 4
+
+
+def sends(source, hop, chips):
+    target = source + hop
+    direct = needed(source, target) & ((target != EDGE) | (hop == EDGE - RELAY))
+    return (target < chips) & (direct | ((source == EDGE - 1) & (hop == 2)))
 
 
 def kernel(
     chips, group, flags_ref, x_ref, wk_ref, wv_ref, cos_ref, sin_ref, freq_ref, wq_hbm, out_hbm,
-    kv, send, xs, wq, queries, top, mix, bias_own, blocked, staged, cosine, sine,
-    wq_sem, x_send, x_recv, kv_send, kv_recv, out_sem, out_send, out_recv,
+    kv, send, xs, wq, queries, top, mix, bias_own, onehot, blocked, staged, cosine, sine,
+    wq_sem, x_send, x_recv, kv_send, kv_recv, relay_send, out_sem, out_send, out_recv,
 ):
     me = lax.axis_index("ctx")
     chip, core = me // 2, me % 2
@@ -32,6 +43,7 @@
     sibling = chip * 2 + other
     tok = x_ref.shape[0]
     half = wq.shape[1]
+    tiles = 2 * tok // TILE
     scale = math.log2(math.e) / math.sqrt(HEAD)
 
     wq_copy = pltpu.make_async_copy(
@@ -42,13 +54,17 @@
     barrier = pltpu.get_barrier_semaphore()
     pl.semaphore_signal(barrier, inc=1, device_id={"ctx": sibling})
     for hop in range(1, 5):
-        @pl.when(needed(chip - hop, chip))
+        @pl.when((chip >= hop) & sends(chip - hop, hop, chips))
         def _():
             for c in range(2) if hop < 4 else (1,):
                 pl.semaphore_signal(barrier, inc=1, device_id={"ctx": (chip - hop) * 2 + c})
 
+    @pl.when(chip == EDGE)
+    def _():
+        pl.semaphore_signal(barrier, inc=1, device_id={"ctx": (EDGE + 1) * 2 + core})
+
     def sends_to(hop):
-        fits = (chip + hop < chips) & needed(chip, chip + hop)
+        fits = sends(chip, hop, chips)
         return fits if hop < 4 else fits & (core == 1)
 
     base = (chip * (2 * tok)).astype(jnp.float32) * freq_ref[...]
@@ -73,12 +89,14 @@
         vs = jnp.dot(x, wv_ref[:, cols], preferred_element_type=jnp.float32)
         for h in range(heads):
             hc = slice(h * HEAD, (h + 1) * HEAD)
-            send[part, 2 * h * tok:(2 * h + 1) * tok, :] = rope(ks[:, hc], cs, sn).astype(jnp.bfloat16)
+            turned = rope(ks[:, hc], cs, sn).astype(jnp.bfloat16)
+            for t in range(tok // TILE):
+                send[part, 2 * h * tok + t * TILE:2 * h * tok + (t + 1) * TILE, :] = turned[t * TILE:(t + 1) * TILE].T
             send[part, (2 * h + 1) * tok:(2 * h + 2) * tok, :] = vs[:, hc].astype(jnp.bfloat16)
         send[part, 2 * heads * tok:, :] = flag_rows
 
     targets = sum(sends_to(hop).astype(jnp.int32) for hop in range(1, 5))
-    pl.semaphore_wait(barrier, 1 + 2 * targets)
+    pl.semaphore_wait(barrier, 1 + 2 * targets + (chip == EDGE + 1).astype(jnp.int32))
 
     def kv_copy(hop, part):
         return pltpu.make_async_remote_copy(
@@ -87,6 +105,22 @@
             device_id={"ctx": (chip + hop) * 2 + part},
         )
 
+    def relay_copy(index, from_hop, to_hop, c):
+        return pltpu.make_async_remote_copy(
+            src_ref=kv.at[from_hop, c], dst_ref=kv.at[to_hop, c],
+            send_sem=relay_send.at[index], recv_sem=kv_recv.at[to_hop, c],
+            device_id={"ctx": EDGE * 2 + core},
+        )
+
+    def arrived(hop, c):
+        pltpu.make_async_remote_copy(
+            src_ref=send.at[0], dst_ref=kv.at[hop, c], send_sem=kv_send.at[hop, 0],
+            recv_sem=kv_recv.at[hop, c], device_id={"ctx": sibling},
+        ).wait_recv()
+
+    early = ((2, 4, 1), (1, 3, 0), (1, 3, 1))
+    late = ((2, 1, 0), (2, 1, 1))
+
     def own_copy():
         return pltpu.make_async_remote_copy(
             src_ref=send.at[other], dst_ref=kv.at[0, core],
@@ -110,59 +144,67 @@
     x_copy.wait()
     wq_copy.wait()
     pairs = half // (2 * HEAD)
-    tiles = 2 * tok // TILE
 
     @pl.loop(0, pairs)
     def _(pair):
         kvh, hp = pair // (group // 2), pair % (group // 2)
         w = wq[:, pl.ds(pl.multiple_of(pair * 2 * HEAD, 2 * HEAD), 2 * HEAD)]
-        for c in range(2):
-            q = jnp.dot(xs[c], w, preferred_element_type=jnp.float32)
-            for e in range(2):
-                r = rope(
-                    q[:, e * HEAD:(e + 1) * HEAD], cosine[c * tok:(c + 1) * tok, :], sine[c * tok:(c + 1) * tok, :]
-                ).astype(jnp.bfloat16)
-                for t in range(tok // TILE):
-                    queries[
-                        kvh, c * (tok // TILE) + t, pl.ds(pl.multiple_of((hp * 2 + e) * TILE, TILE), TILE), :
-                    ] = r[t * TILE:(t + 1) * TILE]
+        q = jnp.dot(xs[...].reshape(2 * tok, -1), w, preferred_element_type=jnp.float32)
+        for e in range(2):
+            r = rope(q[:, e * HEAD:(e + 1) * HEAD], cosine[...], sine[...]).astype(jnp.bfloat16)
+            for t in range(tiles):
+                queries[kvh, t, pl.ds(pl.multiple_of((hp * 2 + e) * TILE, TILE), TILE), :] = (
+                    r[t * TILE:(t + 1) * TILE]
+                )
 
     def marks(hop, c):
         rows = kv[hop, c, 2 * heads * tok:, :].astype(jnp.float32)
         return [rows[0:1], rows[MARK_ROWS // 2:MARK_ROWS // 2 + 1]]
 
-    chunk = 2 * TILE
-
-    def attend(hop, unit_tiles, cores, bias_of, first):
-        @pl.loop(0, heads * unit_tiles)
-        def _(unit):
-            h, i = unit // unit_tiles, unit % unit_tiles
-            k0 = pl.multiple_of(h * 2 * tok, tok)
-            v0 = pl.multiple_of(h * 2 * tok + tok, tok)
-            k = jnp.concatenate([kv[hop, c, pl.ds(k0, tok), :] for c in cores], axis=0)
-            v = jnp.concatenate([kv[hop, c, pl.ds(v0, tok), :] for c in cores], axis=0)
-            v = jnp.concatenate([v, jnp.ones_like(v)], axis=1)
-            bias = bias_of(i)
-            for r in range(group * TILE // chunk):
-                rows = slice(r * chunk, (r + 1) * chunk)
-                s = lax.dot_general(
-                    queries[h, i, rows, :], k, (((1,), (1,)), ((), ())), preferred_element_type=jnp.float32
-                )
-                s = s + bias
-                highest = jnp.max(s, axis=1, keepdims=True)
-                if first:
-                    new = jnp.broadcast_to(highest, (chunk, HEAD))
-                else:
-                    old = top[h, i, rows, :]
-                    new = jnp.maximum(old, highest)
-                wide = jnp.concatenate([new] * (s.shape[1] // HEAD), axis=1)
-                p = jnp.exp2((s - wide) * scale).astype(jnp.bfloat16)
-                o = jnp.dot(p, v, preferred_element_type=jnp.float32)
-                if not first:
-                    factor = jnp.exp2((old - new) * scale)
-                    o = o + mix[h, i, rows, :] * jnp.concatenate([factor, factor], axis=1)
-                mix[h, i, rows, :] = o
-                top[h, i, rows, :] = new
+    chunk = CHUNK
+
+    def attend(hop, i, cores, keys, bias, first):
+        def slab(h):
+            k0, v0 = h * 2 * tok, h * 2 * tok + tok
+            k = jnp.concatenate(
+                [kv[hop, c, k0 + t * TILE:k0 + (t + 1) * TILE, :] for c in cores for t in range(tok // TILE)], axis=1
+            )[:, :keys]
+            v = jnp.concatenate([kv[hop, c, v0:v0 + tok, :] for c in cores], axis=0)[:keys]
+            return jnp.concatenate([k, bias], axis=0), jnp.concatenate([v, jnp.ones_like(v)], axis=1)
+
+        slabs = [slab(h) for h in range(heads)]
+        work = [(h, slice(r * chunk, (r + 1) * chunk)) for h in range(heads) for r in range(group * TILE // chunk)]
+
+        def score(h, rows):
+            return jnp.dot(
+                jnp.concatenate([queries[h, i, rows, :], onehot[...]], axis=1), slabs[h][0],
+                preferred_element_type=jnp.float32,
+            )
+
+        ahead = [score(*w) for w in work[:AHEAD]]
+        for n, (h, rows) in enumerate(work):
+            if n + AHEAD < len(work):
+                ahead.append(score(*work[n + AHEAD]))
+            s = ahead[n]
+            highest = jnp.max(s, axis=1, keepdims=True)
+            if first:
+                new = jnp.broadcast_to(highest, (chunk, HEAD))
+            else:
+                old = top[h, i, rows, :]
+                new = jnp.maximum(old, highest)
+            wide = jnp.concatenate([new] * (keys // HEAD), axis=1)
+            p = jnp.exp2((s - wide) * scale).astype(jnp.bfloat16)
+            o = jnp.dot(p, slabs[h][1], preferred_element_type=jnp.float32)
+            if not first:
+                factor = jnp.exp2((old - new) * scale)
+                o = o + mix[h, i, rows, :] * jnp.concatenate([factor, factor], axis=1)
+            mix[h, i, rows, :] = o
+            top[h, i, rows, :] = new
+
+    onehot[...] = jnp.where(
+        lax.broadcasted_iota(jnp.int32, onehot.shape, 0) % TILE == lax.broadcasted_iota(jnp.int32, onehot.shape, 1),
+        1.0, 0.0,
+    ).astype(jnp.bfloat16)
 
     own_copy().wait_send()
     pltpu.make_async_remote_copy(
@@ -171,36 +213,42 @@
     ).wait_recv()
     flags = marks(0, 0) + marks(0, 1)
     row = lax.broadcasted_iota(jnp.int32, (TILE, TILE), 0)
-    col = lax.broadcasted_iota(jnp.int32, (TILE, TILE), 1)
-    causal = jnp.where(col <= row, 0.0, NEG)
+    key = lax.broadcasted_iota(jnp.int32, (TILE, TILE), 1)
+    causal = jnp.where(key <= row, 0.0, NEG).astype(jnp.bfloat16)
     for i in range(tiles):
-        seen = jnp.zeros((1, HEAD), jnp.float32)
-        for j in reversed(range(tiles)):
-            cols = slice(j * TILE, (j + 1) * TILE)
-            if j > i:
-                bias_own[i, :, cols] = jnp.full((TILE, TILE), NEG, jnp.float32)
-            elif j == i:
-                bias_own[i, :, cols] = causal
-                seen = flags[j]
-            else:
-                bias_own[i, :, cols] = jnp.broadcast_to(seen * NEG, (TILE, TILE))
-                seen = jnp.maximum(seen, flags[j])
+        seen = flags[i]
+        bias_own[i, :, i * TILE:(i + 1) * TILE] = causal
+        for j in reversed(range(i)):
+            bias_own[i, :, j * TILE:(j + 1) * TILE] = jnp.broadcast_to(seen * NEG, (TILE, TILE)).astype(jnp.bfloat16)
+            seen = jnp.maximum(seen, flags[j])
         blocked[i] = jnp.broadcast_to(seen, (8, HEAD))
 
-    def own_bias(i):
-        b = bias_own[i]
-        return jnp.concatenate([b] * (chunk // TILE), axis=0)
-
-    attend(0, tiles, (0, 1), own_bias, True)
+    for i in range(tiles):
+        keys = (i + 1) * TILE
+
+        attend(0, i, (0, 1), keys, bias_own[i, :, :keys], True)
+
+    @pl.when(chip == EDGE - RELAY)
+    def _():
+        for index, (here, there, c) in enumerate(early):
+            arrived(here, c)
+            relay_copy(index, here, there, c).start()
+        arrived(2, 0)
+
+    @pl.when(chip == EDGE + 1)
+    def _():
+        for index, (here, there, c) in enumerate(late):
+            arrived(here, c)
+            relay_copy(index, here, there, c).start()
 
     def far_bias(i, cores, hop):
         seen = blocked[i][0:1]
-        cols = []
+        blocks = []
         for c in reversed(cores):
             for f in reversed(marks(hop, c)):
-                cols.insert(0, seen * NEG)
+                blocks.insert(0, jnp.broadcast_to(seen * NEG, (TILE, HEAD)).astype(jnp.bfloat16))
                 seen = jnp.maximum(seen, f)
-        return jnp.concatenate(cols, axis=1), seen
+        return jnp.concatenate(blocks, axis=1), seen
 
     for hop in range(1, 5):
         cores = (0, 1) if hop < 4 else (1,)
@@ -208,12 +256,16 @@
 
         @pl.when(needed(chip - hop, chip))
         def _():
-            for c in cores:
-                pltpu.make_async_remote_copy(
-                    src_ref=send.at[0], dst_ref=kv.at[hop, c], send_sem=kv_send.at[hop, 0],
-                    recv_sem=kv_recv.at[hop, c], device_id={"ctx": sibling},
-                ).wait_recv()
-            attend(hop, unit_tiles, cores, lambda i: far_bias(i, cores, hop)[0], False)
+            @pl.when((chip != EDGE - RELAY) | (hop > 2))
+            def _():
+                for c in cores:
+                    arrived(hop, c)
+
+
+            @pl.loop(0, jnp.where(chip == EDGE, 1, unit_tiles))
+            def _(i):
+                attend(hop, i, cores, len(cores) * tok, far_bias(i, cores, hop)[0], False)
+
             if hop < 4:
                 for i in range(tiles):
                     blocked[i] = jnp.broadcast_to(far_bias(i, cores, hop)[1], (8, HEAD))
@@ -243,6 +295,11 @@
         def _():
             for part in range(2):
                 kv_copy(hop, part).wait_send()
+    for role, moves in ((EDGE - RELAY, early), (EDGE + 1, late)):
+        @pl.when(chip == role)
+        def _():
+            for index, (here, there, c) in enumerate(moves):
+                relay_copy(index, here, there, c).wait_send()
     out_local.wait()
     out_remote.wait()
 
@@ -275,12 +332,13 @@
             pltpu.VMEM((heads, tiles, group * TILE, HEAD), bf),
             pltpu.VMEM((heads, tiles, group * TILE, HEAD), f32),
             pltpu.VMEM((heads, tiles, group * TILE, 2 * HEAD), f32),
-            pltpu.VMEM((tiles, TILE, tiles * TILE), f32),
+            pltpu.VMEM((tiles, TILE, tiles * TILE), bf),
+            pltpu.VMEM((CHUNK, TILE), bf),
             pltpu.VMEM((tiles, 8, HEAD), f32),
             pltpu.VMEM((2 * tok, half), bf),
             pltpu.VMEM((2 * tok, HEAD), f32),
             pltpu.VMEM((2 * tok, HEAD), f32),
-            dma, dma, dma, dma((5, 2)), dma((5, 2)), dma, dma, dma,
+            dma, dma, dma, dma((5, 2)), dma((5, 2)), dma((3,)), dma, dma, dma,
         ],
         compiler_params=pltpu.CompilerParams(
             collective_id=0, has_side_effects=True, vmem_limit_bytes=56 * 1024 * 1024

time: 58.1 us -> 46.9 us (0.81)
  the two profiles are of different devices: /device:TPU:17 before, /device:TPU:31 now
where the time goes in v2:
time: 46.9 us; the launch traced here: 46.7 us
  Pallas kernels  43.6 us (93%)
  local copies, waits for them, and re-layouts  3.13 us (7%)
    pallas_call x1, Pallas kernels, local(): pl.pallas_call(functools.partial(kernel, chips, group), out_shape=jax.Sha...  43.6 us
    unnamed x1, local copies, waits for them, and re-layouts  3.13 us

profile of v2, /device:TPU:31, one launch (start us, length us, event | category | flops | bytes accessed | tf_op | source)
XLA Modules:
  0.0 46.7 jit_solution(1369329896798504774)
XLA Ops:
  0.0 43.6 %shard_map.82 = bf16[256,4096]{1,0:T(8,128)(2,1)} custom-call(s32[2]{0:T(128)} %flags_ref.1, bf16[256,1024]{1,0:T(8,128)(2,1)} %x_ref.1, bf16[1024,512]{1,0:T(8,128)(2,1)} %wk_ref.1, bf16[1024,512]{1,0:T(8,128)(2,1)} %wv_ref.1, f32[512,128]{1,0:T(8,128)} %constant.6.clone.cos_ref, f32[512,128]{1,0:T(8,128)} %constant.7.clone.sin_ref, ...), custom_call_target="tpu_custom_call" | custom-call | flops 12000000000 | bytes 12000000 | tf_op jit(solution)/shard_map/pallas_call | solution.py:322
  43.6 3.1 %copy.10 = bf16[256,4096]{1,0:T(8,128)(2,1)} copy(bf16[256,4096]{1,0:T(8,128)(2,1)} %shard_map.82) | data formatting | bytes 4194304
